TPU v7x, 32 devices: a whole 2x2x4 slice. The times are simulated.
32 devices in a mesh: fsdp: 2 (over x), heads: 4 (over z), tensor: 4 (over y, core).
Axes of the slice: x: 2, y: 2, z: 4, core: 2. Of those that a mesh axis runs over, the one named last changes fastest.
Arguments:
- latent_tokens: bfloat16 [16, 1024, 1152], P('fsdp', ('heads', 'tensor')), may hold values from -6 to 6
- labels: int32 [16], replicated, may hold values from 0 to 999
- timesteps: int32 [16], replicated, may hold values from 0 to 999
- class_table: bfloat16 [1000, 1152], P(None, 'fsdp'), may hold values from -6 to 6
- time_table: bfloat16 [1000, 1152], P(None, 'fsdp'), may hold values from -6 to 6
- ada_weight: bfloat16 [1152, 6912], P(('fsdp', 'heads'), 'tensor'), may hold values from -0.1875 to 0.1875
- ada_bias: bfloat16 [6912], P('tensor'), may hold values from -3 to 3
- qkv_weight: bfloat16 [1152, 3, 1152], P(('fsdp', 'heads'), None, 'tensor'), may hold values from -0.1875 to 0.1875
- qkv_bias: bfloat16 [3, 1152], P(None, 'tensor'), may hold values from -3 to 3
- proj_weight: bfloat16 [1152, 1152], P('tensor', ('fsdp', 'heads')), may hold values from -1.5 to 1.5
- proj_bias: bfloat16 [1152], replicated, may hold values from -3 to 3
- up_weight: bfloat16 [1152, 4608], P(('fsdp', 'heads'), 'tensor'), may hold values from -0.1875 to 0.1875
- up_bias: bfloat16 [4608], P('tensor'), may hold values from -3 to 3
- down_weight: bfloat16 [4608, 1152], P('tensor', ('fsdp', 'heads')), may hold values from -0.09375 to 0.09375
- down_bias: bfloat16 [1152], replicated, may hold values from -3 to 3
- cotangent: bfloat16 [16, 1024, 1152], P('fsdp', ('heads', 'tensor')), may hold values from -6 to 6
Outputs:
- block_out: bfloat16 [16, 1024, 1152], P('fsdp', ('heads', 'tensor'))
- grad_tokens: bfloat16 [16, 1024, 1152], P('fsdp', ('heads', 'tensor'))
- grad_class_table: float32 [1000, 1152], P(None, 'fsdp')
- grad_time_table: float32 [1000, 1152], P(None, 'fsdp')
- grad_ada_weight: float32 [1152, 6912], P(('fsdp', 'heads'), 'tensor')
- grad_ada_bias: float32 [6912], P('tensor')
- grad_qkv_weight: float32 [1152, 3, 1152], P(('fsdp', 'heads'), None, 'tensor')
- grad_qkv_bias: float32 [3, 1152], P(None, 'tensor')
- grad_proj_weight: float32 [1152, 1152], P('tensor', ('fsdp', 'heads'))
- grad_proj_bias: float32 [1152], replicated
- grad_up_weight: float32 [1152, 4608], P(('fsdp', 'heads'), 'tensor')
- grad_up_bias: float32 [4608], P('tensor')
- grad_down_weight: float32 [4608, 1152], P('tensor', ('fsdp', 'heads'))
- grad_down_bias: float32 [1152], replicated
All inputs are finite; a program needn't handle non-finite values.
Results may differ from a plain program's by a relative error of at most 0.018.
The roundings to bfloat16 on the way count: a program that leaves them out, or rounds other values in their place, can miss the bound.
Values may be sent and summed in bfloat16 or wider, within the bound.
A program may use at most 192 MiB of HBM per device.

v0:
```python
import jax
import jax.numpy as jnp
from jax import lax
from jax.sharding import PartitionSpec as P

HEAD_DIM = 72


layer_eps = 1e-06


def norm_rows(values):
    centre = values - jnp.mean(values, axis=-1, keepdims=True)
    spread = jnp.mean(centre * centre, axis=-1, keepdims=True)
    return centre * lax.rsqrt(spread + layer_eps)


def gelu_tanh(values):
    return jax.nn.gelu(values, approximate=True)


def tensor_rows(values):
    return lax.all_gather(values, "tensor", axis=1, tiled=True)


def tensor_sums(values):
    return lax.psum_scatter(values, "tensor", scatter_dimension=1, tiled=True)


def to_heads(values):
    return lax.all_to_all(values, "heads", split_axis=3, concat_axis=1, tiled=True)


def to_tokens(values):
    return lax.all_to_all(values, "heads", split_axis=1, concat_axis=3, tiled=True)


def choose_rows(indices, count):
    return indices[:, None] == lax.broadcasted_iota(jnp.int32, (indices.shape[0], count), 1)


def attend_one(block):
    factor = block.shape[-1] ** (-0.5)
    queries, keys_in, values_in = (block[:, 0], block[:, 1], block[:, 2])
    scores = (
        jnp.einsum("qhe,khe->hqk", queries, keys_in, preferred_element_type=jnp.float32) * factor
    )
    highest = jnp.max(scores, axis=-1, keepdims=True)
    raised = jnp.exp(scores - highest)
    summed = jnp.sum(raised, axis=-1, keepdims=True)
    weights = (raised / summed).astype(jnp.bfloat16)
    result = jnp.einsum("hqk,khe->qhe", weights, values_in, preferred_element_type=jnp.float32)
    return (result.astype(jnp.bfloat16), (highest + jnp.log(summed))[..., 0])


def attend_back(items):
    block, log_total, grad_out = items
    factor = block.shape[-1] ** (-0.5)
    queries, keys_in, values_in = (block[:, 0], block[:, 1], block[:, 2])
    scores = (
        jnp.einsum("qhe,khe->hqk", queries, keys_in, preferred_element_type=jnp.float32) * factor
    )
    probs = jnp.exp(scores - log_total[..., None])
    grad_values = jnp.einsum(
        "hqk,qhe->khe", probs.astype(jnp.bfloat16), grad_out, preferred_element_type=jnp.float32
    )
    grad_probs = jnp.einsum("qhe,khe->hqk", grad_out, values_in, preferred_element_type=jnp.float32)
    centred = jnp.sum(grad_probs * probs, axis=-1, keepdims=True)
    grad_scores = (probs * (grad_probs - centred)).astype(jnp.bfloat16)
    grad_queries = (
        jnp.einsum("hqk,khe->qhe", grad_scores, keys_in, preferred_element_type=jnp.float32)
        * factor
    )
    grad_keys = (
        jnp.einsum("hqk,qhe->khe", grad_scores, queries, preferred_element_type=jnp.float32)
        * factor
    )
    return jnp.stack([grad_queries, grad_keys, grad_values], axis=1).astype(jnp.bfloat16)


def shards(
    latent_tokens,
    labels,
    timesteps,
    class_table,
    time_table,
    ada_weight,
    ada_bias,
    qkv_weight,
    qkv_bias,
    proj_weight,
    proj_bias,
    up_weight,
    up_bias,
    down_weight,
    down_bias,
    cotangent,
):
    latents_here = latent_tokens.shape[0]
    model_width = latent_tokens.shape[2]
    all_latents = labels.shape[0]
    fsdp_rank = lax.axis_index("fsdp")
    head_rank = lax.axis_index("heads")
    tensor_rank = lax.axis_index("tensor")
    ada_columns = ada_bias.shape[0]
    qkv_columns = qkv_bias.shape[1]
    up_columns = up_bias.shape[0]
    per_tensor = qkv_columns // HEAD_DIM
    gathered = (
        lax.all_gather(ada_weight, ("fsdp", "heads"), axis=0, tiled=True),
        lax.all_gather(qkv_weight, ("fsdp", "heads"), axis=0, tiled=True),
        lax.all_gather(proj_weight, ("fsdp", "heads"), axis=1, tiled=True),
        lax.all_gather(up_weight, ("fsdp", "heads"), axis=0, tiled=True),
        lax.all_gather(down_weight, ("fsdp", "heads"), axis=1, tiled=True),
    )
    ada_whole, qkv_whole, projection_weight_gathered, up_weight_gathered, down_weight_gathered = (
        gathered
    )
    class_pick = choose_rows(labels, class_table.shape[0])
    time_pick = choose_rows(timesteps, time_table.shape[0])
    cond_part = jnp.dot(
        class_pick.astype(jnp.bfloat16), class_table, preferred_element_type=jnp.float32
    ) + jnp.dot(time_pick.astype(jnp.bfloat16), time_table, preferred_element_type=jnp.float32)
    cond_all = lax.all_gather(cond_part, "fsdp", axis=1, tiled=True)
    condition = lax.dynamic_slice_in_dim(cond_all, fsdp_rank * latents_here, latents_here, 0)
    lifted_wide, silu_back = jax.vjp(jax.nn.silu, condition)
    lifted = lifted_wide.astype(jnp.bfloat16)
    ada_part = jnp.dot(lifted, ada_whole, preferred_element_type=jnp.float32) + ada_bias
    modulation = lax.all_gather(ada_part, "tensor", axis=1, tiled=True)
    pieces = [
        modulation[:, None, position * model_width : (position + 1) * model_width]
        for position in range(6)
    ]
    shift_first, scale_first, gate_first, shift_second, scale_second, gate_second = pieces
    residual_in = latent_tokens.astype(jnp.float32)
    normed_first, norm_back_first = jax.vjp(norm_rows, residual_in)
    input_first = (normed_first * (1.0 + scale_first) + shift_first).astype(jnp.bfloat16)
    rows_first = tensor_rows(input_first)
    group_rows = rows_first.shape[1]
    qkv_local = (
        jnp.einsum("lsd,dce->lsce", rows_first, qkv_whole, preferred_element_type=jnp.float32)
        + qkv_bias
    ).astype(jnp.bfloat16)
    grouped = qkv_local.reshape(latents_here, group_rows, 3, per_tensor, HEAD_DIM)
    by_heads = to_heads(grouped)
    attention_output, log_total = lax.map(attend_one, by_heads)
    modulated_tokens = to_tokens(attention_output[:, :, None]).reshape(
        latents_here, group_rows, qkv_columns
    )
    attention_branch = (
        tensor_sums(
            jnp.einsum(
                "tpz,zm->tpm",
                modulated_tokens,
                projection_weight_gathered,
                preferred_element_type=jnp.float32,
            )
        )
        + proj_bias
    )
    middle = residual_in + gate_first * attention_branch
    normed_second, norm_back_second = jax.vjp(norm_rows, middle)
    feedforward_input = (normed_second * (1.0 + scale_second) + shift_second).astype(jnp.bfloat16)
    second_token_rows = tensor_rows(feedforward_input)
    preactivation = (
        jnp.einsum(
            "vyg,gq->vyq", second_token_rows, up_weight_gathered, preferred_element_type=jnp.float32
        )
        + up_bias
    )
    activated_wide, gelu_back = jax.vjp(gelu_tanh, preactivation)
    gelu_activations = activated_wide.astype(jnp.bfloat16)
    feedforward_branch = (
        tensor_sums(
            jnp.einsum(
                "tpz,zm->tpm",
                gelu_activations,
                down_weight_gathered,
                preferred_element_type=jnp.float32,
            )
        )
        + down_bias
    )
    block_out = (middle + gate_second * feedforward_branch).astype(jnp.bfloat16)
    backward_set = (
        lax.all_gather(ada_weight, ("fsdp", "heads"), axis=0, tiled=True),
        lax.all_gather(qkv_weight, ("fsdp", "heads"), axis=0, tiled=True),
        lax.all_gather(proj_weight, ("fsdp", "heads"), axis=1, tiled=True),
        lax.all_gather(up_weight, ("fsdp", "heads"), axis=0, tiled=True),
        lax.all_gather(down_weight, ("fsdp", "heads"), axis=1, tiled=True),
    )
    ada_whole, qkv_whole, projection_weight_gathered, up_weight_gathered, down_weight_gathered = (
        backward_set
    )
    grad_out = cotangent.astype(jnp.float32)
    grad_branch_second = (grad_out * gate_second).astype(jnp.bfloat16)
    gate_second_sum = jnp.sum(grad_out * feedforward_branch, axis=1)
    second_row_gradient = tensor_rows(grad_branch_second)
    down_grad = jnp.einsum(
        "egr,egh->rh", gelu_activations, second_row_gradient, preferred_element_type=jnp.float32
    )
    grad_act = jnp.einsum(
        "xjw,mw->xjm", second_row_gradient, down_weight_gathered, preferred_element_type=jnp.float32
    )
    grad_preactivation = gelu_back(grad_act)[0].astype(jnp.bfloat16)
    upward_gradient = jnp.einsum(
        "box,bor->xr", second_token_rows, grad_preactivation, preferred_element_type=jnp.float32
    )
    grad_input_second = tensor_sums(
        jnp.einsum(
            "rqt,xt->rqx",
            grad_preactivation,
            up_weight_gathered,
            preferred_element_type=jnp.float32,
        )
    )
    up_bias_full = lax.dynamic_update_slice(
        jnp.zeros((up_columns * lax.axis_size("tensor"),), jnp.float32),
        jnp.sum(grad_preactivation.astype(jnp.float32), axis=(0, 1)),
        (tensor_rank * up_columns,),
    )
    shift_second_sum = jnp.sum(grad_input_second, axis=1)
    scale_second_sum = jnp.sum(grad_input_second * normed_second, axis=1)
    grad_middle = grad_out + norm_back_second(grad_input_second * (1.0 + scale_second))[0]
    grad_branch_first = (grad_middle * gate_first).astype(jnp.bfloat16)
    gate_first_sum = jnp.sum(grad_middle * attention_branch, axis=1)
    first_row_gradient = tensor_rows(grad_branch_first)
    proj_grad = jnp.einsum(
        "egr,egh->rh", modulated_tokens, first_row_gradient, preferred_element_type=jnp.float32
    )
    grad_mixed = jnp.einsum(
        "xjw,mw->xjm",
        first_row_gradient,
        projection_weight_gathered,
        preferred_element_type=jnp.float32,
    ).astype(jnp.bfloat16)
    grad_heads = to_heads(grad_mixed.reshape(latents_here, group_rows, 1, per_tensor, HEAD_DIM))[
        :, :, 0
    ]
    grad_blocks = lax.map(attend_back, (by_heads, log_total, grad_heads))
    grad_qkv = to_tokens(grad_blocks).reshape(latents_here, group_rows, 3, qkv_columns)
    qkv_grad = jnp.einsum("lsd,lsce->dce", rows_first, grad_qkv, preferred_element_type=jnp.float32)
    grad_input_first = tensor_sums(
        jnp.einsum("lsce,dce->lsd", grad_qkv, qkv_whole, preferred_element_type=jnp.float32)
    )
    shift_first_sum = jnp.sum(grad_input_first, axis=1)
    scale_first_sum = jnp.sum(grad_input_first * normed_first, axis=1)
    grad_tokens = (grad_middle + norm_back_first(grad_input_first * (1.0 + scale_first))[0]).astype(
        jnp.bfloat16
    )
    modul_part = jnp.concatenate(
        [
            shift_first_sum,
            scale_first_sum,
            gate_first_sum,
            shift_second_sum,
            scale_second_sum,
            gate_second_sum,
        ],
        axis=1,
    )
    modul_grad = lax.psum(modul_part.astype(jnp.bfloat16), ("heads", "tensor"))
    own_columns = lax.dynamic_slice_in_dim(modul_grad, tensor_rank * ada_columns, ada_columns, 1)
    first_head = (head_rank == 0).astype(jnp.float32)
    first_pair = first_head * (tensor_rank == 0).astype(jnp.float32)
    ada_grad = (
        jnp.einsum("ld,lc->dc", lifted, own_columns, preferred_element_type=jnp.float32)
        * first_head
    )
    lifted_grad = jnp.einsum(
        "lc,dc->ld", own_columns, ada_whole, preferred_element_type=jnp.float32
    )
    cond_grad = silu_back(lifted_grad)[0] * first_head
    cond_padded = lax.dynamic_update_slice(
        jnp.zeros((all_latents, model_width), jnp.float32), cond_grad, (fsdp_rank * latents_here, 0)
    )
    ada_bias_part = jnp.sum(modul_grad.astype(jnp.float32), axis=0) * first_pair
    qkv_bias_full = lax.dynamic_update_slice(
        jnp.zeros((3, model_width), jnp.float32),
        jnp.sum(grad_qkv.astype(jnp.float32), axis=(0, 1)),
        (0, tensor_rank * qkv_columns),
    )
    proj_bias_part = jnp.sum(grad_branch_first.astype(jnp.float32), axis=(0, 1))
    down_bias_part = jnp.sum(grad_branch_second.astype(jnp.float32), axis=(0, 1))
    summed = lax.psum(
        (cond_padded, ada_bias_part, qkv_bias_full, proj_bias_part, up_bias_full, down_bias_part),
        ("fsdp", "heads", "tensor"),
    )
    table_columns = class_table.shape[1]
    cond_columns = lax.dynamic_slice_in_dim(summed[0], fsdp_rank * table_columns, table_columns, 1)
    class_grad = jnp.dot(
        class_pick.astype(jnp.float32).T, cond_columns, precision=lax.Precision.HIGHEST
    )
    time_grad = jnp.dot(
        time_pick.astype(jnp.float32).T, cond_columns, precision=lax.Precision.HIGHEST
    )
    ada_bias_grad = lax.dynamic_slice_in_dim(summed[1], tensor_rank * ada_columns, ada_columns, 0)
    qkv_bias_grad = lax.dynamic_slice_in_dim(summed[2], tensor_rank * qkv_columns, qkv_columns, 1)
    up_bias_grad = lax.dynamic_slice_in_dim(summed[4], tensor_rank * up_columns, up_columns, 0)
    ada_owned, qkv_owned, proj_owned, up_owned, down_owned = (
        lax.psum_scatter(ada_grad, ("fsdp", "heads"), scatter_dimension=0, tiled=True),
        lax.psum_scatter(qkv_grad, ("fsdp", "heads"), scatter_dimension=0, tiled=True),
        lax.psum_scatter(proj_grad, ("fsdp", "heads"), scatter_dimension=1, tiled=True),
        lax.psum_scatter(upward_gradient, ("fsdp", "heads"), scatter_dimension=0, tiled=True),
        lax.psum_scatter(down_grad, ("fsdp", "heads"), scatter_dimension=1, tiled=True),
    )
    return (
        block_out,
        grad_tokens,
        class_grad,
        time_grad,
        ada_owned,
        ada_bias_grad,
        qkv_owned,
        qkv_bias_grad,
        proj_owned,
        summed[3],
        up_owned,
        up_bias_grad,
        down_owned,
        summed[5],
    )


def solution(mesh):
    in_specs = (
        P("fsdp", ("heads", "tensor"), None),
        P(),
        P(),
        P(None, "fsdp"),
        P(None, "fsdp"),
        P(("fsdp", "heads"), "tensor"),
        P("tensor"),
        P(("fsdp", "heads"), None, "tensor"),
        P(None, "tensor"),
        P("tensor", ("fsdp", "heads")),
        P(),
        P(("fsdp", "heads"), "tensor"),
        P("tensor"),
        P("tensor", ("fsdp", "heads")),
        P(),
        P("fsdp", ("heads", "tensor"), None),
    )
    out_specs = (
        P("fsdp", ("heads", "tensor"), None),
        P("fsdp", ("heads", "tensor"), None),
        P(None, "fsdp"),
        P(None, "fsdp"),
        P(("fsdp", "heads"), "tensor"),
        P("tensor"),
        P(("fsdp", "heads"), None, "tensor"),
        P(None, "tensor"),
        P("tensor", ("fsdp", "heads")),
        P(),
        P(("fsdp", "heads"), "tensor"),
        P("tensor"),
        P("tensor", ("fsdp", "heads")),
        P(),
    )
    return jax.shard_map(shards, mesh=mesh, in_specs=in_specs, out_specs=out_specs, check_vma=False)
```

profile of v0, /device:TPU:0, one launch (start us, length us, event | category | flops | bytes accessed | tf_op | source)
XLA Modules:
  0.0 2168.4 jit_solution(11897682504833565476)
XLA Ops:
  19.3 66.2 %all-gather.11.cloned.1.call-done = bf16[1152,1728]{1,0:T(8,128)(2,1)} async-done(((bf16[144,1728]{1,0:T(8,128)(2,1)}), bf16[1152,1728]{1,0:T(8,128)(2,1)}) %all-gather.11.cloned.1.call-update) | async-done | bytes 3981328 | tf_op jit(solution)/shard_map/all_gather | solution.py:110
  97.3 43.7 %all-gather.15.cloned.1.call-done = bf16[1152,3,288]{2,0,1:T(8,128)(2,1)} async-done(((bf16[144,3,288]{2,0,1:T(8,128)(2,1)}), bf16[1152,3,288]{2,0,1:T(8,128)(2,1)}) %all-gather.15.cloned.1.call-update) | async-done | bytes 1990672 | tf_op jit(solution)/shard_map/all_gather | solution.py:111
  141.1 38.2 %all-gather.13.cloned.1.call-done = bf16[8,256,1152]{2,1,0:T(8,128)(2,1)} async-done(((bf16[8,64,1152]{2,1,0:T(8,128)(2,1)}), bf16[8,256,1152]{2,1,0:T(8,128)(2,1)}) %all-gather.13.cloned.1.call-update) | async-done | bytes 4718608 | tf_op jit(solution)/shard_map/all_gather | solution.py:23
  194.0 79.8 %all-to-all-done = bf16[8,256,3,4,72]{1,4,2,0,3:T(8,128)(2,1)} async-done(((bf16[8,256,3,4,72]{1,4,2,0,3:T(8,128)(2,1)}), bf16[8,256,3,4,72]{1,4,2,0,3:T(8,128)(2,1)}, u32[]{:S(2)}, u32[]{:S(2)}) %all-to-all-start) | async-done | bytes 3538976 | tf_op jit(solution)/shard_map/all_to_all | solution.py:31
  278.1 32.9 %while.22 = (s32[]{:T(128)}, bf16[8,1024,1,72]{1,3,2,0:T(8,128)(2,1)S(1)}, f32[8,1,1024]{2,1,0:T(1,128)}, bf16[8,1024,3,1,72]{1,4,3,2,0:T(8,128)(2,1)}, s32[]{:T(128)}) while((s32[]{:T(128)}, bf16[8,1024,1,72]{1,3,2,0:T(8,128)(2,1)S(1)}, f32[8,1,1024]{2,1,0:T(1,128)}, bf16[8,1024,3,1,72]{1,4,3,2,0:T(8,128)(2,1)}, s32[]{:T(128)}) %tuple.120), condition=%wide.region_5.6_spmd, body=%wide.region_2.5_spmd.sunk | while | flops 311499776 | bytes 14098513 | solution.py:146
  317.6 78.0 %all_gather.43 = bf16[288,1152]{0,1:T(8,128)(2,1)} all-gather(bf16[288,144]{0,1:T(8,128)(2,1)S(1)} %copy-done.20), channel_id=1, replica_groups=mesh['fsdp'=2,'heads'=4,'tensor'=4] {'fsdp','heads'}, dimensions={1}, use_global_device_ids=true | all-gather | bytes 746496 | tf_op jit(solution)/shard_map/all_gather | solution.py:112
  406.8 76.8 %reduce-scatter.10.cloned.1.call-done = f32[8,64,1152]{2,1,0:T(8,128)} async-done(((f32[8,256,1152]{2,1,0:T(8,128)}), f32[8,64,1152]{2,1,0:T(8,128)}) %reduce-scatter.10.cloned.1.call-update) | async-done | bytes 2359312 | tf_op jit(solution)/shard_map/reduce_scatter | solution.py:27
  491.9 48.6 %all-gather.19.cloned.1.call-done = bf16[1152,1152]{1,0:T(8,128)(2,1)} async-done(((bf16[144,1152]{1,0:T(8,128)(2,1)}), bf16[1152,1152]{1,0:T(8,128)(2,1)}) %all-gather.19.cloned.1.call-update) | async-done | bytes 2654224 | tf_op jit(solution)/shard_map/all_gather | solution.py:113
  540.5 38.1 %all-gather.17.cloned.1.call-done = bf16[8,256,1152]{2,1,0:T(8,128)(2,1)} async-done(((bf16[8,64,1152]{2,1,0:T(8,128)(2,1)}), bf16[8,256,1152]{2,1,0:T(8,128)(2,1)}) %all-gather.17.cloned.1.call-update) | async-done | bytes 4718608 | tf_op jit(solution)/shard_map/all_gather | solution.py:23
  578.6 11.7 fusion.54
  590.3 45.5 %all-gather.21.cloned.1.call-done = bf16[1152,1152]{0,1:T(8,128)(2,1)} async-done(((bf16[1152,144]{0,1:T(8,128)(2,1)}), bf16[1152,1152]{0,1:T(8,128)(2,1)}) %all-gather.21.cloned.1.call-update) | async-done | bytes 2654224 | tf_op jit(solution)/shard_map/all_gather | solution.py:114
  635.8 38.2 %all-gather.23.cloned.1.call-done = bf16[8,256,1152]{2,1,0:T(8,128)(2,1)} async-done(((bf16[8,64,1152]{2,1,0:T(8,128)(2,1)}), bf16[8,256,1152]{2,1,0:T(8,128)(2,1)}) %all-gather.23.cloned.1.call-update) | async-done | bytes 4718608 | tf_op jit(solution)/shard_map/all_gather | solution.py:23
  674.0 15.4 convert_reduce_fusion
  701.1 78.3 %reduce-scatter.14.cloned.1.call-done = f32[8,64,1152]{2,1,0:T(8,128)} async-done(((f32[8,256,1152]{2,1,0:T(8,128)}), f32[8,64,1152]{2,1,0:T(8,128)}) %reduce-scatter.14.cloned.1.call-update) | async-done | bytes 2359312 | tf_op jit(solution)/shard_map/reduce_scatter | solution.py:27
  788.7 37.6 %all-gather.25.cloned.1.call-done = bf16[8,256,1152]{2,1,0:T(8,128)(2,1)} async-done(((bf16[8,64,1152]{2,1,0:T(8,128)(2,1)}), bf16[8,256,1152]{2,1,0:T(8,128)(2,1)}) %all-gather.25.cloned.1.call-update) | async-done | bytes 4718608 | tf_op jit(solution)/shard_map/all_gather | solution.py:23
  836.4 28.9 %all-to-all-done.2 = bf16[8,256,1,4,72]{1,4,0,2,3:T(8,128)(2,1)S(1)} async-done(((bf16[8,256,1,4,72]{1,4,0,2,3:T(8,128)(2,1)}), bf16[8,256,1,4,72]{1,4,0,2,3:T(8,128)(2,1)S(1)}, u32[]{:S(2)}, u32[]{:S(2)}) %all-to-all-start.2) | async-done | bytes 1179680 | tf_op jit(solution)/shard_map/all_to_all | solution.py:31
  869.9 61.0 %while.23 = (s32[]{:T(128)}, bf16[8,1024,3,1,72]{1,4,3,2,0:T(8,128)(2,1)}, bf16[8,1024,3,1,72]{1,4,3,2,0:T(8,128)(2,1)}, f32[8,1,1024]{2,1,0:T(1,128)}, bf16[8,1024,1,72]{1,3,2,0:T(8,128)(2,1)S(1)}, /*index=5*/s32[]{:T(128)}) while((s32[]{:T(128)}, bf16[8,1024,3,1,72]{1,4,3,2,0:T(8,128)(2,1)}, bf16[8,1024,3,1,72]{1,4,3,2,0:T(8,128)(2,1)}, ...), condition=%wide.region_15.16_spmd, body=%wide.region_13.15_spmd.sunk | while | flops 769252352 | bytes 34730080 | solution.py:240
  938.9 144.6 %all_to_all.63 = bf16[8,1024,3,1,72]{4,0,3,2,1:T(8,128)(2,1)} all-to-all(bf16[8,1024,3,1,72]{4,0,3,2,1:T(8,128)(2,1)} %copy.116), channel_id=1, replica_groups=mesh['fsdp'=2,'heads'=4,'tensor'=4] {'heads'}, dimensions={1} | all-to-all | bytes 7077888 | tf_op jit(solution)/shard_map/all_to_all | solution.py:35
  1094.6 9.6 convolution_bitcast_fusion.2
  1104.9 14.2 fusion.50
  1122.6 58.3 %reduce-scatter.16.cloned.1.call-done = f32[8,64,1152]{2,1,0:T(8,128)} async-done(((f32[8,256,1152]{2,1,0:T(8,128)}), f32[8,64,1152]{2,1,0:T(8,128)}) %reduce-scatter.16.cloned.1.call-update) | async-done | bytes 2359312 | tf_op jit(solution)/shard_map/reduce_scatter | solution.py:27
  1187.2 74.6 %reduce-scatter.12.cloned.1.call-done = f32[8,64,1152]{2,1,0:T(8,128)} async-done(((f32[8,256,1152]{2,1,0:T(8,128)}), f32[8,64,1152]{2,1,0:T(8,128)}) %reduce-scatter.12.cloned.1.call-update) | async-done | bytes 2359312 | tf_op jit(solution)/shard_map/reduce_scatter | solution.py:27
  1275.0 80.9 %all-reduce.5.cloned.1.call-done = bf16[8,6912]{1,0:T(8,128)(2,1)} async-done(((bf16[8,6912]{1,0:T(8,128)(2,1)}), bf16[8,6912]{1,0:T(8,128)(2,1)}) %all-reduce.5.cloned.1.call-update) | async-done | bytes 110608 | tf_op jit(solution)/shard_map/psum | solution.py:262
  1361.8 12.5 convolution_bitcast_fusion.1
  1375.0 14.0 convolution_bitcast_fusion
  1412.4 75.0 %all-reduce.9.cloned.1.call-done = (f32[6912]{0:T(1024)}, f32[3,1152]{1,0:T(4,128)}, f32[1152]{0:T(1024)}, f32[4608]{0:T(1024)}, f32[1152]{0:T(1024)}) async-done(((f32[6912]{0:T(1024)}, f32[3,1152]{1,0:T(4,128)}, f32[1152]{0:T(1024)}, f32[4608]{0:T(1024)}, f32[1152]{0:T(1024)}), (f32[6912]{0:T(1024)}, f32[3,1152]{1,0:T(4,128)}, f32[1152]{0:T(1024)}, f32[4608]{0:T(1024)}, ...) | async-done | bytes 69136 | tf_op jit(solution)/shard_map/psum | solution.py:285
  1491.5 121.6 %all-reduce.7.cloned.1.call-done = f32[16,1152]{1,0:T(8,128)} async-done(((f32[16,1152]{1,0:T(8,128)}), f32[16,1152]{1,0:T(8,128)}) %all-reduce.7.cloned.1.call-update) | async-done | bytes 73744 | tf_op jit(solution)/shard_map/psum | solution.py:285
  1620.0 103.2 %reduce-scatter.24.cloned.1.call-done = f32[144,1152]{1,0:T(8,128)} async-done(((f32[1152,1152]{1,0:T(8,128)}), f32[144,1152]{1,0:T(8,128)}) %reduce-scatter.24.cloned.1.call-update) | async-done | bytes 663568 | tf_op jit(solution)/shard_map/reduce_scatter | solution.py:304
  1723.2 108.4 %reduce-scatter.26.cloned.1.call-done = f32[1152,144]{0,1:T(8,128)} async-done(((f32[1152,1152]{0,1:T(8,128)}), f32[1152,144]{0,1:T(8,128)}) %reduce-scatter.26.cloned.1.call-update) | async-done | bytes 663568 | tf_op jit(solution)/shard_map/reduce_scatter | solution.py:305
  1831.6 70.1 %reduce-scatter.22.cloned.1.call-done = f32[288,144]{0,1:T(8,128)} async-done(((f32[288,1152]{0,1:T(8,128)}), f32[288,144]{0,1:T(8,128)}) %reduce-scatter.22.cloned.1.call-update) | async-done | bytes 165904 | tf_op jit(solution)/shard_map/reduce_scatter | solution.py:303
  1901.7 107.7 %reduce-scatter.20.cloned.1.call-done = f32[144,3,288]{2,0,1:T(8,128)} async-done(((f32[1152,3,288]{2,0,1:T(8,128)}), f32[144,3,288]{2,0,1:T(8,128)}) %reduce-scatter.20.cloned.1.call-update) | async-done | bytes 497680 | tf_op jit(solution)/shard_map/reduce_scatter | solution.py:302
  2009.4 150.7 %reduce-scatter.18.cloned.1.call-done = f32[144,1728]{1,0:T(8,128)} async-done(((f32[1152,1728]{1,0:T(8,128)}), f32[144,1728]{1,0:T(8,128)}) %reduce-scatter.18.cloned.1.call-update) | async-done | bytes 995344 | tf_op jit(solution)/shard_map/reduce_scatter | solution.py:301
  (333 shorter events, 282.5 us)
Async XLA Ops:
  7.2 78.2 %all-gather.11.cloned.1.call-start = ((), (), s32[]{:S(2)}) async-start(), calls=%async_computation.13 | async-start | bytes 4644864 | tf_op jit(solution)/shard_map/all_gather | solution.py:110
  7.9 133.1 %all-gather.15.cloned.1.call-start = ((), (), s32[]{:S(2)}) async-start(), calls=%async_computation.15 | async-start | bytes 2985984 | tf_op jit(solution)/shard_map/all_gather | solution.py:111
  8.7 170.6 %all-gather.13.cloned.1.call-start = ((), (), s32[]{:S(2)}) async-start(), calls=%async_computation.14 | async-start | bytes 5898240 | tf_op jit(solution)/shard_map/all_gather | solution.py:23
  189.2 84.6 %all-to-all-start = ((bf16[8,256,3,4,72]{1,4,2,0,3:T(8,128)(2,1)}), bf16[8,256,3,4,72]{1,4,2,0,3:T(8,128)(2,1)}, u32[]{:S(2)}, u32[]{:S(2)}) async-start(bf16[8,256,3,4,72]{1,4,2,0,3:T(8,128)(2,1)} %copy.107), calls=%async_computation | async-start | bytes 7077888 | tf_op jit(solution)/shard_map/all_to_all | solution.py:31
  313.8 81.8 %all-to-all-start.1 = ((bf16[8,1024,1,1,72]{4,0,3,2,1:T(8,128)(2,1)}), bf16[8,1024,1,1,72]{4,0,3,2,1:T(8,128)(2,1)S(1)}, u32[]{:S(2)}, u32[]{:S(2)}) async-start(bf16[8,1024,1,1,72]{4,0,3,2,1:T(8,128)(2,1)} %bitcast.234), calls=%async_computation.1 | async-start | bytes 4194304 | tf_op jit(solution)/shard_map/all_to_all | solution.py:35
  317.5 166.0 %reduce-scatter.10.cloned.1.call-start = ((), (), s32[]{:S(2)}) async-start(), calls=%async_computation.16 | async-start | bytes 11796480 | tf_op jit(solution)/shard_map/reduce_scatter | solution.py:27
  406.1 134.5 %all-gather.19.cloned.1.call-start = ((), (), s32[]{:S(2)}) async-start(), calls=%async_computation.18 | async-start | bytes 2985984 | tf_op jit(solution)/shard_map/all_gather | solution.py:113
  406.7 171.9 %all-gather.17.cloned.1.call-start = ((), (), s32[]{:S(2)}) async-start(), calls=%async_computation.17 | async-start | bytes 5898240 | tf_op jit(solution)/shard_map/all_gather | solution.py:23
  406.8 78.9 %copy-start.21 = (f32[1152]{0:T(1024)}, f32[1152]{0:T(1024)S(1)}, u32[]{:S(2)}) copy-start(f32[1152]{0:T(1024)S(1)} %convert_element_type.116) | copy-start | bytes 13828
  487.8 148.0 %all-gather.21.cloned.1.call-start = ((), (), s32[]{:S(2)}) async-start(), calls=%async_computation.19 | async-start | bytes 2985984 | tf_op jit(solution)/shard_map/all_gather | solution.py:114
  488.5 185.5 %all-gather.23.cloned.1.call-start = ((), (), s32[]{:S(2)}) async-start(), calls=%async_computation.21 | async-start | bytes 5898240 | tf_op jit(solution)/shard_map/all_gather | solution.py:23
  491.3 288.1 %reduce-scatter.14.cloned.1.call-start = ((), (), s32[]{:S(2)}) async-start(), calls=%async_computation.22 | async-start | bytes 11796480 | tf_op jit(solution)/shard_map/reduce_scatter | solution.py:27
  700.9 125.5 %all-gather.25.cloned.1.call-start = ((), (), s32[]{:S(2)}) async-start(), calls=%async_computation.23 | async-start | bytes 5898240 | tf_op jit(solution)/shard_map/all_gather | solution.py:23
  831.8 33.5 %all-to-all-start.2 = ((bf16[8,256,1,4,72]{1,4,0,2,3:T(8,128)(2,1)}), bf16[8,256,1,4,72]{1,4,0,2,3:T(8,128)(2,1)S(1)}, u32[]{:S(2)}, u32[]{:S(2)}) async-start(bf16[8,256,1,4,72]{1,4,0,2,3:T(8,128)(2,1)} %copy.112), calls=%async_computation.5 | async-start | bytes 2359296 | tf_op jit(solution)/shard_map/all_to_all | solution.py:31
  836.4 344.5 %reduce-scatter.16.cloned.1.call-start = ((), (), s32[]{:S(2)}) async-start(), calls=%async_computation.24 | async-start | bytes 11796480 | tf_op jit(solution)/shard_map/reduce_scatter | solution.py:27
  1104.2 157.6 %reduce-scatter.12.cloned.1.call-start = ((), (), s32[]{:S(2)}) async-start(), calls=%async_computation.20 | async-start | bytes 11796480 | tf_op jit(solution)/shard_map/reduce_scatter | solution.py:27
  1119.1 236.9 %all-reduce.5.cloned.1.call-start = ((), (), s32[]{:S(2)}) async-start(), calls=%async_computation.25 | async-start | bytes 221184 | tf_op jit(solution)/shard_map/psum | solution.py:262
  1183.3 78.6 %copy-start.22 = (f32[1152]{0:T(1024)S(1)}, f32[1152]{0:T(1024)}, u32[]{:S(2)}) copy-start(f32[1152]{0:T(1024)} %copy-done.21) | copy-start | bytes 13828
  1268.1 89.5 %copy-start.13 = (f32[1152,16]{0,1:T(8,128)S(1)}, f32[1152,16]{0,1:T(8,128)}, u32[]{:S(2)}) copy-start(f32[1152,16]{0,1:T(8,128)} %copy-done.12) | copy-start | bytes 221188
  1270.6 216.7 %all-reduce.9.cloned.1.call-start = ((), (), s32[]{:S(2)}) async-start(), calls=%async_computation.32 | async-start | bytes 167936 | tf_op jit(solution)/shard_map/psum | solution.py:285
  1275.0 82.5 %copy-start.25 = (f32[3,1152]{1,0:T(4,128)}, f32[3,1152]{1,0:T(4,128)S(1)}, u32[]{:S(2)}) copy-start(f32[3,1152]{1,0:T(4,128)S(1)} %dynamic_update_slice.22) | copy-start | bytes 41476
  1357.6 255.5 %all-reduce.7.cloned.1.call-start = ((), (), s32[]{:S(2)}) async-start(), calls=%async_computation.26 | async-start | bytes 147456 | tf_op jit(solution)/shard_map/psum | solution.py:285
  1361.7 361.5 %reduce-scatter.24.cloned.1.call-start = ((), (), s32[]{:S(2)}) async-start(), calls=%async_computation.30 | async-start | bytes 5971968 | tf_op jit(solution)/shard_map/reduce_scatter | solution.py:304
  1374.3 457.3 %reduce-scatter.26.cloned.1.call-start = ((), (), s32[]{:S(2)}) async-start(), calls=%async_computation.31 | async-start | bytes 5971968 | tf_op jit(solution)/shard_map/reduce_scatter | solution.py:305
  1389.0 512.7 %reduce-scatter.22.cloned.1.call-start = ((), (), s32[]{:S(2)}) async-start(), calls=%async_computation.29 | async-start | bytes 1990656 | tf_op jit(solution)/shard_map/reduce_scatter | solution.py:303
  1395.9 613.6 %reduce-scatter.20.cloned.1.call-start = ((), (), s32[]{:S(2)}) async-start(), calls=%async_computation.28 | async-start | bytes 5971968 | tf_op jit(solution)/shard_map/reduce_scatter | solution.py:302
  1406.2 753.9 %reduce-scatter.18.cloned.1.call-start = ((), (), s32[]{:S(2)}) async-start(), calls=%async_computation.27 | async-start | bytes 9289728 | tf_op jit(solution)/shard_map/reduce_scatter | solution.py:301
  1412.4 200.7 %copy-start.39 = (s32[16]{0:T(128)S(1)}, s32[16]{0:T(128)}, u32[]{:S(2)}) copy-start(s32[16]{0:T(128)} %param.22) | copy-start | bytes 196
  1412.4 204.2 %copy-start.40 = (s32[16]{0:T(128)S(1)}, s32[16]{0:T(128)}, u32[]{:S(2)}) copy-start(s32[16]{0:T(128)} %param.21) | copy-start | bytes 196
  1412.4 749.0 %copy-start.1 = (bf16[1000,576]{0,1:T(8,128)(2,1)S(1)}, bf16[1000,576]{0,1:T(8,128)(2,1)}, u32[]{:S(2)}) copy-start(bf16[1000,576]{0,1:T(8,128)(2,1)} %param.23) | copy-start | bytes 3456004
  1487.4 672.8 %copy-start.35 = (f32[1152]{0:T(1024)S(1)}, f32[1152]{0:T(1024)}, u32[]{:S(2)}) copy-start(f32[1152]{0:T(1024)} %get-tuple-element.280) | copy-start | bytes 13828
  1487.4 673.4 %copy-start.34 = (f32[1152]{0:T(1024)S(1)}, f32[1152]{0:T(1024)}, u32[]{:S(2)}) copy-start(f32[1152]{0:T(1024)} %get-tuple-element.284) | copy-start | bytes 13828
  (35 other events, 521.1 us)
Sparse Core Ops, SparseCore 0:
  10.1 75.2 all-gather.10
  87.7 53.3 all-gather.14
  143.2 36.0 all-gather.12
  406.2 77.2 reduce-scatter.9
  485.5 55.0 all-gather.18
  542.5 36.0 all-gather.16
  580.7 55.0 all-gather.20
  637.9 36.0 all-gather.22
  701.0 78.3 reduce-scatter.13
  788.9 37.4 all-gather.24
  1104.3 76.5 reduce-scatter.15
  1183.4 78.4 reduce-scatter.11
  1270.7 85.1 all-reduce.4
  1362.8 124.4 all-reduce.8
  1493.4 119.6 all-reduce.6
  1617.1 106.0 reduce-scatter.23
  1727.6 103.9 reduce-scatter.25
  1835.5 66.2 reduce-scatter.21
  1906.3 103.0 reduce-scatter.19
  2013.6 146.5 reduce-scatter.17
where the time goes:
time: 2180 us; the launch traced here: 2170 us
  waiting for transfers between devices  1570 us (72%)
  blocking collectives  234 us (11%)
  matrix products  189 us (9%)
  local copies, waits for them, and re-layouts  81.7 us (4%)
  other arithmetic  59.9 us (3%)
    reduce_scatter x4, waiting for transfers between devices, tensor_sums(): return lax.psum_scatter(values, 'tensor', scatter_dimension=1, tiled=True)  288 us
    psum x2, waiting for transfers between devices, shards(): lax.psum((cond_padded, ada_bias_part, qkv_bias_full, proj_bias_part, up_b...  197 us
    all_gather x4, waiting for transfers between devices, tensor_rows(): return lax.all_gather(values, 'tensor', axis=1, tiled=True)  152 us
    reduce_scatter x1, waiting for transfers between devices, shards(): lax.psum_scatter(ada_grad, ('fsdp', 'heads'), scatter_dimension=0, tiled=...  151 us
    all_to_all x1, blocking collectives, to_tokens(): lax.all_to_all(values, 'heads', split_axis=1, concat_axis=3, tiled=True)  145 us
    all_to_all x2, waiting for transfers between devices, to_heads(): lax.all_to_all(values, 'heads', split_axis=3, concat_axis=1, tiled=True)  109 us
    reduce_scatter x1, waiting for transfers between devices, shards(): lax.psum_scatter(down_grad, ('fsdp', 'heads'), scatter_dimension=1, tiled...  108 us
    reduce_scatter x1, waiting for transfers between devices, shards(): lax.psum_scatter(qkv_grad, ('fsdp', 'heads'), scatter_dimension=0, tiled=...  108 us
  transfers between devices with their start and end apart: 23, of which 22 were waited for; matrix products, arithmetic and copies ran while one was open for 6% of the time, Pallas kernels for 0%

commit v1 on v0

v1 whole, which is shorter than its diff:
```python
import jax
import jax.numpy as jnp
from jax import lax
from jax.sharding import PartitionSpec as P

HEAD_DIM = 72
GROUP = ("fsdp", "heads")


layer_eps = 1e-06


def norm_rows(values):
    centre = values - jnp.mean(values, axis=-1, keepdims=True)
    spread = jnp.mean(centre * centre, axis=-1, keepdims=True)
    return centre * lax.rsqrt(spread + layer_eps)


def gelu_tanh(values):
    return jax.nn.gelu(values, approximate=True)


def tensor_rows(values):
    return lax.all_gather(values, "tensor", axis=1, tiled=True)


def tensor_sums(values):
    return lax.psum_scatter(
        values.astype(jnp.bfloat16), "tensor", scatter_dimension=1, tiled=True
    ).astype(jnp.float32)


def to_owner(values):
    return lax.all_to_all(values, "heads", split_axis=0, concat_axis=1, tiled=True)


def to_tokens(values):
    return lax.all_to_all(values, "heads", split_axis=1, concat_axis=0, tiled=True)


def choose_rows(indices, count):
    return indices[:, None] == lax.broadcasted_iota(jnp.int32, (indices.shape[0], count), 1)


def attend_one(items):
    queries, keys_in, values_in = items
    factor = queries.shape[-1] ** (-0.5)
    scores = jnp.einsum("qe,ke->qk", queries, keys_in, preferred_element_type=jnp.float32) * factor
    highest = jnp.max(scores, axis=-1, keepdims=True)
    raised = jnp.exp(scores - highest)
    summed = jnp.sum(raised, axis=-1, keepdims=True)
    weights = (raised / summed).astype(jnp.bfloat16)
    result = jnp.einsum("qk,ke->qe", weights, values_in, preferred_element_type=jnp.float32)
    return (result.astype(jnp.bfloat16), (highest + jnp.log(summed))[..., 0])


def attend_back(items):
    queries, keys_in, values_in, log_total, grad_out = items
    factor = queries.shape[-1] ** (-0.5)
    scores = jnp.einsum("qe,ke->qk", queries, keys_in, preferred_element_type=jnp.float32) * factor
    probs = jnp.exp(scores - log_total[..., None])
    grad_values = jnp.einsum(
        "qk,qe->ke", probs.astype(jnp.bfloat16), grad_out, preferred_element_type=jnp.float32
    )
    grad_probs = jnp.einsum("qe,ke->qk", grad_out, values_in, preferred_element_type=jnp.float32)
    centred = jnp.sum(grad_probs * probs, axis=-1, keepdims=True)
    grad_scores = (probs * (grad_probs - centred)).astype(jnp.bfloat16)
    grad_queries = (
        jnp.einsum("qk,ke->qe", grad_scores, keys_in, preferred_element_type=jnp.float32) * factor
    )
    grad_keys = (
        jnp.einsum("qk,qe->ke", grad_scores, queries, preferred_element_type=jnp.float32) * factor
    )
    return tuple(v.astype(jnp.bfloat16) for v in (grad_queries, grad_keys, grad_values))


def product(formula, left, right):
    return jnp.einsum(formula, left, right, preferred_element_type=jnp.float32)


def owned_sum(values, dimension):
    return lax.psum_scatter(
        values.astype(jnp.bfloat16), GROUP, scatter_dimension=dimension, tiled=True
    ).astype(jnp.float32)


def shards(
    latent_tokens,
    labels,
    timesteps,
    class_table,
    time_table,
    ada_weight,
    ada_bias,
    qkv_weight,
    qkv_bias,
    proj_weight,
    proj_bias,
    up_weight,
    up_bias,
    down_weight,
    down_bias,
    cotangent,
):
    model_width = latent_tokens.shape[2]
    all_latents = labels.shape[0]
    head_rank = lax.axis_index("heads")
    tensor_size = lax.axis_size("tensor")
    head_size = lax.axis_size("heads")
    group_size = lax.axis_size("fsdp") * head_size
    own_latents = all_latents // group_size
    ada_rows, ada_columns = ada_weight.shape
    qkv_columns = qkv_bias.shape[1]
    up_columns = up_bias.shape[0]
    per_tensor = qkv_columns // HEAD_DIM

    qkv_whole = lax.all_gather(qkv_weight, GROUP, axis=0, tiled=True)
    residual_in = to_owner(latent_tokens).astype(jnp.float32)

    class_pick = choose_rows(labels, class_table.shape[0])
    time_pick = choose_rows(timesteps, time_table.shape[0])
    condition = product("ac,cd->ad", class_pick.astype(jnp.bfloat16), class_table) + product(
        "ac,cd->ad", time_pick.astype(jnp.bfloat16), time_table
    )
    lifted_wide, silu_back = jax.vjp(jax.nn.silu, condition)
    lifted = lax.dynamic_slice_in_dim(lifted_wide, head_rank * ada_rows, ada_rows, 1).astype(
        jnp.bfloat16
    )
    ada_part = product("ar,rc->ac", lifted, ada_weight)
    ada_part = lax.all_to_all(ada_part, GROUP, split_axis=0, concat_axis=0, tiled=True)
    ada_own = jnp.sum(ada_part.reshape(group_size, own_latents, ada_columns), axis=0) + ada_bias
    modulation = lax.all_gather(ada_own, "tensor", axis=1, tiled=True)
    pieces = [
        modulation[:, None, position * model_width : (position + 1) * model_width]
        for position in range(6)
    ]
    shift_first, scale_first, gate_first, shift_second, scale_second, gate_second = pieces

    normed_first, norm_back_first = jax.vjp(norm_rows, residual_in)
    input_first = (normed_first * (1.0 + scale_first) + shift_first).astype(jnp.bfloat16)
    rows_first = tensor_rows(input_first)
    sequence = rows_first.shape[1]
    proj_whole = lax.all_gather(proj_weight, GROUP, axis=1, tiled=True)
    up_whole = lax.all_gather(up_weight, GROUP, axis=0, tiled=True)
    down_whole = lax.all_gather(down_weight, GROUP, axis=1, tiled=True)

    def split_heads(values):
        cut = values.reshape(own_latents, sequence, per_tensor, HEAD_DIM)
        return cut.transpose(0, 2, 1, 3).reshape(own_latents * per_tensor, sequence, HEAD_DIM)

    def join_heads(values):
        cut = values.reshape(own_latents, per_tensor, sequence, HEAD_DIM)
        return cut.transpose(0, 2, 1, 3).reshape(own_latents, sequence, qkv_columns)

    qkv_local = (product("lsd,dce->lsce", rows_first, qkv_whole) + qkv_bias).astype(jnp.bfloat16)
    queries, keys_in, values_in = (split_heads(qkv_local[:, :, index]) for index in range(3))
    attention_output, log_total = lax.map(attend_one, (queries, keys_in, values_in))
    mixed = join_heads(attention_output)
    attention_branch = tensor_sums(product("tpz,zm->tpm", mixed, proj_whole)) + proj_bias
    middle = residual_in + gate_first * attention_branch
    normed_second, norm_back_second = jax.vjp(norm_rows, middle)
    input_second = (normed_second * (1.0 + scale_second) + shift_second).astype(jnp.bfloat16)
    rows_second = tensor_rows(input_second)
    preactivation = product("vyg,gq->vyq", rows_second, up_whole) + up_bias
    activated_wide, gelu_back = jax.vjp(gelu_tanh, preactivation)
    activated = activated_wide.astype(jnp.bfloat16)
    feedforward_branch = tensor_sums(product("tpz,zm->tpm", activated, down_whole)) + down_bias
    block_out = to_tokens((middle + gate_second * feedforward_branch).astype(jnp.bfloat16))

    grad_out = to_owner(cotangent).astype(jnp.float32)
    grad_branch_second = (grad_out * gate_second).astype(jnp.bfloat16)
    gate_second_sum = jnp.sum(grad_out * feedforward_branch, axis=1)
    second_rows = tensor_rows(grad_branch_second)
    down_owned = owned_sum(product("egr,egh->rh", activated, second_rows), 1)
    grad_act = product("xjw,mw->xjm", second_rows, down_whole)
    grad_preactivation = gelu_back(grad_act)[0].astype(jnp.bfloat16)
    up_owned = owned_sum(product("box,bor->xr", rows_second, grad_preactivation), 0)
    grad_input_second = tensor_sums(product("rqt,xt->rqx", grad_preactivation, up_whole))
    shift_second_sum = jnp.sum(grad_input_second, axis=1)
    scale_second_sum = jnp.sum(grad_input_second * normed_second, axis=1)
    grad_middle = grad_out + norm_back_second(grad_input_second * (1.0 + scale_second))[0]
    grad_branch_first = (grad_middle * gate_first).astype(jnp.bfloat16)
    gate_first_sum = jnp.sum(grad_middle * attention_branch, axis=1)
    first_rows = tensor_rows(grad_branch_first)
    proj_owned = owned_sum(product("egr,egh->rh", mixed, first_rows), 1)
    grad_mixed = split_heads(product("xjw,mw->xjm", first_rows, proj_whole).astype(jnp.bfloat16))
    grad_heads = lax.map(attend_back, (queries, keys_in, values_in, log_total, grad_mixed))
    grad_qkv = jnp.stack([join_heads(values) for values in grad_heads], axis=2)
    qkv_owned = owned_sum(product("lsd,lsce->dce", rows_first, grad_qkv), 0)
    grad_input_first = tensor_sums(product("lsce,dce->lsd", grad_qkv, qkv_whole))
    shift_first_sum = jnp.sum(grad_input_first, axis=1)
    scale_first_sum = jnp.sum(grad_input_first * normed_first, axis=1)
    grad_tokens = to_tokens(
        (grad_middle + norm_back_first(grad_input_first * (1.0 + scale_first))[0]).astype(
            jnp.bfloat16
        )
    )

    modul_part = jnp.concatenate(
        [
            shift_first_sum,
            scale_first_sum,
            gate_first_sum,
            shift_second_sum,
            scale_second_sum,
            gate_second_sum,
        ],
        axis=1,
    ).reshape(own_latents, tensor_size, ada_columns)
    modul_part = lax.all_to_all(modul_part, "tensor", split_axis=1, concat_axis=1, tiled=True)
    modul_own = jnp.sum(modul_part, axis=1).astype(jnp.bfloat16)
    modul_grad = lax.all_gather(modul_own, GROUP, axis=0, tiled=True)
    ada_grad = product("ar,ac->rc", lifted, modul_grad)
    ada_bias_grad = jnp.sum(modul_grad.astype(jnp.float32), axis=0)
    lifted_grad = lax.all_gather(
        product("ac,rc->ar", modul_grad, ada_weight), ("heads", "tensor"), axis=0
    )
    lifted_grad = jnp.sum(lifted_grad.reshape(head_size, tensor_size, all_latents, ada_rows), axis=1)
    lifted_grad = lifted_grad.transpose(1, 0, 2).reshape(all_latents, head_size * ada_rows)
    cond_columns = silu_back(lifted_grad)[0]
    class_grad = jnp.dot(
        class_pick.astype(jnp.float32).T, cond_columns, precision=lax.Precision.HIGHEST
    )
    time_grad = jnp.dot(
        time_pick.astype(jnp.float32).T, cond_columns, precision=lax.Precision.HIGHEST
    )

    bias_part = jnp.concatenate(
        [
            jnp.sum(grad_qkv.astype(jnp.float32), axis=(0, 1)).reshape(-1),
            jnp.sum(grad_preactivation.astype(jnp.float32), axis=(0, 1)),
            jnp.sum(first_rows.astype(jnp.float32), axis=(0, 1)),
            jnp.sum(second_rows.astype(jnp.float32), axis=(0, 1)),
        ]
    )
    bias_part = jnp.pad(bias_part, (0, -bias_part.shape[0] % 1024)).reshape(1, -1, 128)
    bias_sums = jnp.sum(lax.all_gather(bias_part, GROUP, axis=0, tiled=True), axis=0).reshape(-1)
    first_cut = 3 * qkv_columns
    second_cut = first_cut + up_columns
    third_cut = second_cut + model_width
    return (
        block_out,
        grad_tokens,
        class_grad,
        time_grad,
        ada_grad,
        ada_bias_grad,
        qkv_owned,
        bias_sums[:first_cut].reshape(3, qkv_columns),
        proj_owned,
        bias_sums[second_cut:third_cut],
        up_owned,
        bias_sums[first_cut:second_cut],
        down_owned,
        bias_sums[third_cut : third_cut + model_width],
    )


def solution(mesh):
    in_specs = (
        P("fsdp", ("heads", "tensor"), None),
        P(),
        P(),
        P(None, "fsdp"),
        P(None, "fsdp"),
        P(("fsdp", "heads"), "tensor"),
        P("tensor"),
        P(("fsdp", "heads"), None, "tensor"),
        P(None, "tensor"),
        P("tensor", ("fsdp", "heads")),
        P(),
        P(("fsdp", "heads"), "tensor"),
        P("tensor"),
        P("tensor", ("fsdp", "heads")),
        P(),
        P("fsdp", ("heads", "tensor"), None),
    )
    out_specs = (
        P("fsdp", ("heads", "tensor"), None),
        P("fsdp", ("heads", "tensor"), None),
        P(None, "fsdp"),
        P(None, "fsdp"),
        P(("fsdp", "heads"), "tensor"),
        P("tensor"),
        P(("fsdp", "heads"), None, "tensor"),
        P(None, "tensor"),
        P("tensor", ("fsdp", "heads")),
        P(),
        P(("fsdp", "heads"), "tensor"),
        P("tensor"),
        P("tensor", ("fsdp", "heads")),
        P(),
    )
    return jax.shard_map(shards, mesh=mesh, in_specs=in_specs, out_specs=out_specs, check_vma=False)
```

time: 2180 us -> 1070 us (0.49)
  waiting for transfers between devices: 1570 us -> 465 us
  matrix products: 189 us -> 236 us
  blocking collectives: 234 us -> 205 us
    reduce_scatter x9 -> x8, waiting for transfers between devices: 828 us -> 243 us  [the longest x4 148 us: tensor_sums(): lax.psum_scatter(values.astype(jnp.bfloat16), 'tensor', scatter_dimension...]
    psum x3 -> x0, waiting for transfers between devices: 277 us -> none  [the longest x2 197 us: shards(): lax.psum((cond_padded, ada_bias_part, qkv_bias_full, proj_bias_part, up_b...]
    all_gather x4 -> x3, waiting for transfers between devices: 204 us -> 67 us  [the longest x1 45.5 us: shards(): down_whole = lax.all_gather(down_weight, GROUP, axis=1, tiled=True)]
    all_to_all x1 -> x2, blocking collectives: 145 us -> 58.2 us  [the longest x1 43.7 us: to_owner(): lax.all_to_all(values, 'heads', split_axis=0, concat_axis=1, tiled=True)]
    all_to_all x3 -> x4, waiting for transfers between devices: 109 us -> 31.2 us  [the longest x1 31.2 us: to_owner(): lax.all_to_all(values, 'heads', split_axis=0, concat_axis=1, tiled=True)]
    all_gather x3 -> x5, blocking collectives: 89.4 us -> 146 us  [the longest x1 49.6 us: shards(): lax.all_gather(bias_part, GROUP, axis=0, tiled=True)]
    dot_general x73, matrix products: 182 us -> 231 us  [the longest x17 129 us: product(): return jnp.einsum(formula, left, right, preferred_element_type=jnp.float32)]
    all_gather x4, waiting for transfers between devices: 152 us -> 122 us  [tensor_rows(): return lax.all_gather(values, 'tensor', axis=1, tiled=True)]
  transfers between devices with their start and end apart: 23 -> 19, of which waited for: 22 -> 13; matrix products, arithmetic and copies ran while one was open for 6% -> 23% of each run, Pallas kernels for 0% -> 0%
where the time goes in v1:
time: 1070 us
  waiting for transfers between devices  465 us (43%)
  matrix products  236 us (22%)
  blocking collectives  205 us (19%)
  local copies, waits for them, and re-layouts  62.6 us (6%)
  other arithmetic  62.1 us (6%)
  starting transfers between devices  18.9 us (2%)
  between operations  15.1 us (1%)
    reduce_scatter x4, waiting for transfers between devices, tensor_sums(): lax.psum_scatter(values.astype(jnp.bfloat16), 'tensor', scatter_dimension...  148 us
    dot_general x17, matrix products, product(): return jnp.einsum(formula, left, right, preferred_element_type=jnp.float32)  129 us
    all_gather x4, waiting for transfers between devices, tensor_rows(): return lax.all_gather(values, 'tensor', axis=1, tiled=True)  122 us
    reduce_scatter x4, waiting for transfers between devices, owned_sum(): lax.psum_scatter(values.astype(jnp.bfloat16), GROUP, scatter_dimension=di...  95.3 us
    all_gather x1, blocking collectives, shards(): lax.all_gather(bias_part, GROUP, axis=0, tiled=True)  49.6 us
    all_gather x1, waiting for transfers between devices, shards(): down_whole = lax.all_gather(down_weight, GROUP, axis=1, tiled=True)  45.5 us
    all_to_all x1, blocking collectives, to_owner(): lax.all_to_all(values, 'heads', split_axis=0, concat_axis=1, tiled=True)  43.7 us
    all_gather x1, blocking collectives, shards(): proj_whole = lax.all_gather(proj_weight, GROUP, axis=1, tiled=True)  40.5 us
  transfers between devices with their start and end apart: 19, of which 13 were waited for; matrix products, arithmetic and copies ran while one was open for 23% of the time, Pallas kernels for 0%

profile of v1, /device:TPU:0, one launch (start us, length us, event | category | flops | bytes accessed | tf_op | source)
XLA Modules:
  0.0 1065.1 jit_solution(11610164556004304752)
XLA Ops:
  11.7 14.4 %all_to_all.68 = f32[8,2,1728]{2,1,0:T(2,128)S(1)} all-to-all(f32[8,2,1728]{2,1,0:T(2,128)S(1)} %all_to_all.50), channel_id=1, replica_groups=mesh['fsdp'=2,'heads'=4,'tensor'=4] {'fsdp','heads'}, dimensions={0} | all-to-all | bytes 221184 | tf_op jit(solution)/shard_map/all_to_all | solution.py:130
  36.6 31.2 %all-to-all-done = bf16[8,64,1152]{2,1,0:T(8,128)(2,1)S(1)} async-done(((bf16[8,64,1152]{2,1,0:T(8,128)(2,1)}), bf16[8,64,1152]{2,1,0:T(8,128)(2,1)S(1)}, u32[]{:S(2)}, u32[]{:S(2)}) %all-to-all-start) | async-done | bytes 1179680 | tf_op jit(solution)/shard_map/all_to_all | solution.py:34
  74.3 40.5 %all_gather.42 = bf16[288,1152]{0,1:T(8,128)(2,1)} all-gather(bf16[288,144]{0,1:T(8,128)(2,1)S(1)} %copy-done.27), channel_id=1, replica_groups=mesh['fsdp'=2,'heads'=4,'tensor'=4] {'fsdp','heads'}, dimensions={1}, use_global_device_ids=true | all-gather | bytes 746496 | tf_op jit(solution)/shard_map/all_gather | solution.py:143
  114.8 34.0 %all-gather.11.cloned.1.call-done = bf16[2,1024,1152]{2,1,0:T(8,128)(2,1)} async-done(((bf16[2,256,1152]{2,1,0:T(8,128)(2,1)}), bf16[2,1024,1152]{2,1,0:T(8,128)(2,1)}) %all-gather.11.cloned.1.call-update) | async-done | bytes 4718608 | tf_op jit(solution)/shard_map/all_gather | solution.py:24
  148.9 8.0 add_convert_fusion
  168.4 46.8 %while.26 = (s32[]{:T(128)}, bf16[8,1024,72]{1,2,0:T(8,128)(2,1)S(1)}, f32[8,1024]{1,0:T(8,128)}, bf16[8,1024,72]{2,1,0:T(8,128)(2,1)}, bf16[8,1024,72]{2,1,0:T(...) while((s32[]{:T(128)}, bf16[8,1024,72]{1,2,0:T(8,128)(2,1)S(1)}, f32[8,1024]{1,0:T(8,128)}, ...), condition=%wide.region_6.7_spmd, body=%wide.region_3.6_spmd.sunk | while | flops 311499776 | bytes 13559905 | solution.py:157
  215.2 6.1 convolution_convert_fusion.2
  222.1 47.3 %reduce-scatter.9.cloned.1.call-done = bf16[2,256,1152]{2,1,0:T(8,128)(2,1)} async-done(((bf16[2,1024,1152]{2,1,0:T(8,128)(2,1)}), bf16[2,256,1152]{2,1,0:T(8,128)(2,1)}) %reduce-scatter.9.cloned.1.call-update) | async-done | bytes 1179664 | tf_op jit(solution)/shard_map/reduce_scatter | solution.py:28
  274.7 43.7 %all_to_all.69 = bf16[8,64,1152]{2,1,0:T(8,128)(2,1)S(1)} all-to-all(bf16[8,64,1152]{2,1,0:T(8,128)(2,1)S(1)} %copy-done.19), channel_id=1, replica_groups=mesh['fsdp'=2,'heads'=4,'tensor'=4] {'heads'}, dimensions={0} | all-to-all | bytes 2359296 | tf_op jit(solution)/shard_map/all_to_all | solution.py:34
  321.3 21.5 %all-gather.17.cloned.1.call-done = bf16[1152,1152]{1,0:T(8,128)(2,1)} async-done(((bf16[144,1152]{1,0:T(8,128)(2,1)}), bf16[1152,1152]{1,0:T(8,128)(2,1)}) %all-gather.17.cloned.1.call-update) | async-done | bytes 2654224 | tf_op jit(solution)/shard_map/all_gather | solution.py:144
  342.8 38.1 %all-gather.15.cloned.1.call-done = bf16[2,1024,1152]{2,1,0:T(8,128)(2,1)} async-done(((bf16[2,256,1152]{2,1,0:T(8,128)(2,1)}), bf16[2,1024,1152]{2,1,0:T(8,128)(2,1)}) %all-gather.15.cloned.1.call-update) | async-done | bytes 4718608 | tf_op jit(solution)/shard_map/all_gather | solution.py:24
  380.9 11.7 %fusion.78 = f32[2,1024,1152]{2,1,0:T(8,128)} fusion(bf16[2,1024,1152]{2,1,0:T(8,128)(2,1)} %all-gather.15.cloned.1.call-done, bf16[1152,1152]{1,0:T(8,128)(2,1)} %all-gather.17.cloned.1.call-done), kind=kOutput, calls=%fused_computation.104 | convolution fusion | flops 5435817984 | bytes 16809984 | tf_op jit(solution)/shard_map/vyg,gq->vyq/dot_general | solution.py:78
  392.6 45.5 %all-gather.19.cloned.1.call-done = bf16[1152,1152]{0,1:T(8,128)(2,1)} async-done(((bf16[1152,144]{0,1:T(8,128)(2,1)}), bf16[1152,1152]{0,1:T(8,128)(2,1)}) %all-gather.19.cloned.1.call-update) | async-done | bytes 2654224 | tf_op jit(solution)/shard_map/all_gather | solution.py:145
  438.1 38.3 %all-gather.21.cloned.1.call-done = bf16[2,1024,1152]{2,1,0:T(8,128)(2,1)} async-done(((bf16[2,256,1152]{2,1,0:T(8,128)(2,1)}), bf16[2,1024,1152]{2,1,0:T(8,128)(2,1)}) %all-gather.21.cloned.1.call-update) | async-done | bytes 4718608 | tf_op jit(solution)/shard_map/all_gather | solution.py:24
  476.4 15.3 %convert_reduce_fusion.2 = (f32[1152]{0:T(1024)}, bf16[2,1024,1152]{2,1,0:T(8,128)(2,1)S(1)}) fusion(f32[2,1024,1152]{2,1,0:T(8,128)} %fusion.78, f32[1152]{0:T(1024)S(1)} %convert_element_type.185, bf16[2,1024,1152]{2,1,0:T(8,128)(2,1)} %all-gather.21.cloned.1.call-done, bf16[1152,1152]{0,1:T(8,128)(2,1)} %all-gather.19.cloned.1.call-done), kind=kOutput, calls=%fused_computation.70 | convolution fusion | flops 5490080768 | bytes 21537792 | tf_op jit(solution)/shard_map/xjw,mw->xjm/dot_general | solution.py:78
  493.8 10.4 convolution_convert_fusion
  504.5 13.3 %convolution_convert_fusion.1 = bf16[2,1024,1152]{2,1,0:T(8,128)(2,1)} fusion(bf16[1152,1152]{0,1:T(8,128)(2,1)} %all-gather.19.cloned.1.call-done, f32[2,1024,1152]{2,1,0:T(8,128)} %fusion.78, f32[1152]{0:T(1024)S(1)} %convert_element_type.185), kind=kOutput, calls=%fused_computation.79 | convolution fusion | flops 5461770240 | bytes 16814592 | tf_op jit(solution)/shard_map/tpz,zm->tpm/dot_general | solution.py:78
  519.1 33.1 %reduce-scatter.13.cloned.1.call-done = bf16[2,256,1152]{2,1,0:T(8,128)(2,1)} async-done(((bf16[2,1024,1152]{2,1,0:T(8,128)(2,1)}), bf16[2,256,1152]{2,1,0:T(8,128)(2,1)}) %reduce-scatter.13.cloned.1.call-update) | async-done | bytes 1179664 | tf_op jit(solution)/shard_map/reduce_scatter | solution.py:28
  558.2 44.4 %reduce-scatter.11.cloned.1.call-done = bf16[2,256,1152]{2,1,0:T(8,128)(2,1)} async-done(((bf16[2,1024,1152]{2,1,0:T(8,128)(2,1)}), bf16[2,256,1152]{2,1,0:T(8,128)(2,1)}) %reduce-scatter.11.cloned.1.call-update) | async-done | bytes 1179664 | tf_op jit(solution)/shard_map/reduce_scatter | solution.py:28
  610.6 11.6 %fusion.62 = bf16[1152,1152]{1,0:T(8,128)(2,1)} fusion(bf16[2,1024,1152]{2,1,0:T(8,128)(2,1)} %all-gather.15.cloned.1.call-done, bf16[2,1024,1152]{2,1,0:T(8,128)(2,1)} %copy-done.61), kind=kOutput, calls=%fused_computation.74 | convolution fusion | flops 5437145088 | bytes 12091392 | tf_op jit(solution)/shard_map/box,bor->xr/dot_general | solution.py:78
  622.9 13.4 %fusion.63 = bf16[1152,1152]{0,1:T(8,128)(2,1)} fusion(bf16[2,1024,1152]{2,1,0:T(8,128)(2,1)} %all-gather.21.cloned.1.call-done, f32[2,1024,1152]{2,1,0:T(8,128)} %fusion.78, f32[1152]{0:T(1024)S(1)} %copy-done.53), kind=kOutput, calls=%fused_computation.75 | convolution fusion | flops 5460738048 | bytes 16814592 | tf_op jit(solution)/shard_map/egr,egh->rh/dot_general | solution.py:78
  636.6 11.1 %all-gather.23.cloned.1.call-done = bf16[2,1024,1152]{2,1,0:T(8,128)(2,1)} async-done(((bf16[2,256,1152]{2,1,0:T(8,128)(2,1)}), bf16[2,1024,1152]{2,1,0:T(8,128)(2,1)}) %all-gather.23.cloned.1.call-update) | async-done | bytes 4718608 | tf_op jit(solution)/shard_map/all_gather | solution.py:24
  656.1 88.2 %while.27 = (s32[]{:T(128)}, bf16[8,1024,72]{1,2,0:T(8,128)(2,1)}, bf16[8,1024,72]{1,2,0:T(8,128)(2,1)}, bf16[8,1024,72]{1,2,0:T(8,128)(2,1)S(1)}, bf16[8,1024,7...) while((s32[]{:T(128)}, bf16[8,1024,72]{1,2,0:T(8,128)(2,1)}, ...), condition=%wide.region_16.17_spmd, body=%wide.region_14.16_spmd.sunk | while | flops 767925248 | bytes 33768560 | solution.py:187
  744.3 11.3 %bitcast_convert_fusion = bf16[2,1024,1152]{2,1,0:T(8,128)(2,1)} fusion(bf16[1152,3,288]{2,0,1:T(8,128)(2,1)} %all-gather.13.cloned.1.call-done, bf16[2,1024,1,288]{1,3,2,0:T(8,128)(2,1)S(1)} %bitcast.274, bf16[2,1024,1,288]{1,3,2,0:T(8,128)(2,1)} %bitcast.277, bf16[2,1024,1,288]{1,3,2,0:T(8,128)(2,1)} %bitcast.280), kind=kOutput, calls=%fused_computation.67 | convolution fusion | flops 4082761728 | bytes 10248192 | tf_op jit(solution)/shard_map/lsce,dce->lsd/dot_general | solution.py:78
  769.6 35.2 %reduce-scatter.23.cloned.1.call-done = bf16[1152,144]{0,1:T(8,128)(2,1)} async-done(((bf16[1152,1152]{0,1:T(8,128)(2,1)}), bf16[1152,144]{0,1:T(8,128)(2,1)}) %reduce-scatter.23.cloned.1.call-update) | async-done | bytes 331792 | tf_op jit(solution)/shard_map/reduce_scatter | solution.py:82
  807.9 6.4 fusion.74
  814.4 11.9 %bitcast_convert_fusion.1 = bf16[1152,3,288]{2,0,1:T(8,128)(2,1)} fusion(bf16[2,1024,1152]{2,1,0:T(8,128)(2,1)} %all-gather.11.cloned.1.call-done, bf16[2,1024,1,288]{1,3,2,0:T(8,128)(2,1)S(1)} %bitcast.275, bf16[2,1024,1,288]{1,3,2,0:T(8,128)(2,1)S(1)} %bitcast.278, bf16[2,1024,1,288]{1,3,2,0:T(8,128)(2,1)S(1)} %bitcast.282), kind=kOutput, calls=%fused_computation.81 | convolution fusion | flops 4088475648 | bytes 10248192 | tf_op jit(solution)/shard_map/lsd,lsce->dce/dot_general | solution.py:78
  830.2 23.2 %reduce-scatter.15.cloned.1.call-done = bf16[2,256,1152]{2,1,0:T(8,128)(2,1)} async-done(((bf16[2,1024,1152]{2,1,0:T(8,128)(2,1)}), bf16[2,256,1152]{2,1,0:T(8,128)(2,1)}) %reduce-scatter.15.cloned.1.call-update) | async-done | bytes 1179664 | tf_op jit(solution)/shard_map/reduce_scatter | solution.py:28
  881.9 49.6 %all_gather.51 = f32[8,40,128]{2,1,0:T(8,128)S(1)} all-gather(f32[1,40,128]{2,1,0:T(8,128)S(1)} %pad_bitcast_fusion), channel_id=1, replica_groups=mesh['fsdp'=2,'heads'=4,'tensor'=4] {'fsdp','heads'}, dimensions={0}, use_global_device_ids=true | all-gather | bytes 184320 | tf_op jit(solution)/shard_map/all_gather | solution.py:237
  934.5 60.0 %reduce-scatter.17.cloned.1.call-done = bf16[144,3,288]{2,0,1:T(8,128)(2,1)} async-done(((bf16[1152,3,288]{2,0,1:T(8,128)(2,1)}), bf16[144,3,288]{2,0,1:T(8,128)(2,1)}) %reduce-scatter.17.cloned.1.call-update) | async-done | bytes 248848 | tf_op jit(solution)/shard_map/reduce_scatter | solution.py:82
  997.2 30.7 %all-gather.2 = bf16[8,2,1728]{2,1,0:T(2,128)(2,1)S(1)} all-gather(bf16[1,2,1728]{2,1,0:T(2,128)(2,1)S(1)} %bitcast.296), channel_id=1, replica_groups=mesh['fsdp'=2,'heads'=4,'tensor'=4] {'fsdp','heads'}, dimensions={0}, use_global_device_ids=true | all-gather | bytes 62208 | tf_op jit(solution)/shard_map/all_gather | solution.py:212
  1029.2 20.4 %all-gather = f32[256,144]{1,0:T(8,128)S(1)} all-gather(f32[16,144]{1,0:T(8,128)S(1)} %fusion.117), channel_id=2, replica_groups=mesh['fsdp'=2,'heads'=4,'tensor'=4] {'heads','tensor'}, dimensions={0}, use_global_device_ids=true | all-gather | bytes 156672 | tf_op jit(solution)/shard_map/all_gather | solution.py:215
  (353 shorter events, 267.8 us)
Async XLA Ops:
  26.2 41.6 %all-to-all-start = ((bf16[8,64,1152]{2,1,0:T(8,128)(2,1)}), bf16[8,64,1152]{2,1,0:T(8,128)(2,1)S(1)}, u32[]{:S(2)}, u32[]{:S(2)}) async-start(bf16[8,64,1152]{2,1,0:T(8,128)(2,1)} %param.20), calls=%async_computation | async-start | bytes 2359296 | tf_op jit(solution)/shard_map/all_to_all | solution.py:34
  29.7 85.1 %all-gather.13.cloned.1.call-start = ((), (), s32[]{:S(2)}) async-start(), calls=%async_computation.15 | async-start | bytes 2985984 | tf_op jit(solution)/shard_map/all_gather | solution.py:117
  30.4 118.4 %all-gather.11.cloned.1.call-start = ((), (), s32[]{:S(2)}) async-start(), calls=%async_computation.14 | async-start | bytes 5898240 | tf_op jit(solution)/shard_map/all_gather | solution.py:24
  36.6 36.1 %copy-start.24 = (f32[2,1152]{1,0:T(2,128)}, f32[2,1152]{1,0:T(2,128)S(1)}, u32[]{:S(2)}) copy-start(f32[2,1152]{1,0:T(2,128)S(1)} %get-tuple-element.185) | copy-start | bytes 27652
  68.0 201.4 %copy-start.2 = (f32[4,2,64,1152]{3,2,0,1:T(8,128)}, f32[4,2,64,1152]{3,2,0,1:T(8,128)S(1)}, u32[]{:S(2)}) copy-start(f32[4,2,64,1152]{3,2,0,1:T(8,128)S(1)} %copy.73) | copy-start | bytes 7077892
  74.2 195.1 %reduce-scatter.9.cloned.1.call-start = ((), (), s32[]{:S(2)}) async-start(), calls=%async_computation.16 | async-start | bytes 5898240 | tf_op jit(solution)/shard_map/reduce_scatter | solution.py:28
  221.4 48.0 %copy-start.28 = (f32[2,1152]{1,0:T(2,128)S(1)}, f32[2,1152]{1,0:T(2,128)}, u32[]{:S(2)}) copy-start(f32[2,1152]{1,0:T(2,128)} %get-tuple-element.186) | copy-start | bytes 27652
  221.4 121.4 %all-gather.17.cloned.1.call-start = ((), (), s32[]{:S(2)}) async-start(), calls=%async_computation.18 | async-start | bytes 2985984 | tf_op jit(solution)/shard_map/all_gather | solution.py:144
  222.0 158.9 %all-gather.15.cloned.1.call-start = ((), (), s32[]{:S(2)}) async-start(), calls=%async_computation.17 | async-start | bytes 5898240 | tf_op jit(solution)/shard_map/all_gather | solution.py:24
  222.0 49.1 %copy-start.31 = (f32[1152]{0:T(1024)}, f32[1152]{0:T(1024)S(1)}, u32[]{:S(2)}) copy-start(f32[1152]{0:T(1024)S(1)} %convert_element_type.183) | copy-start | bytes 13828
  274.1 164.1 %all-gather.19.cloned.1.call-start = ((), (), s32[]{:S(2)}) async-start(), calls=%async_computation.19 | async-start | bytes 2985984 | tf_op jit(solution)/shard_map/all_gather | solution.py:145
  274.7 201.8 %all-gather.21.cloned.1.call-start = ((), (), s32[]{:S(2)}) async-start(), calls=%async_computation.21 | async-start | bytes 5898240 | tf_op jit(solution)/shard_map/all_gather | solution.py:24
  321.2 231.0 %reduce-scatter.13.cloned.1.call-start = ((), (), s32[]{:S(2)}) async-start(), calls=%async_computation.22 | async-start | bytes 5898240 | tf_op jit(solution)/shard_map/reduce_scatter | solution.py:28
  321.3 183.2 %copy-start.52 = (f32[1152]{0:T(1024)}, f32[1152]{0:T(1024)S(1)}, u32[]{:S(2)}) copy-start(f32[1152]{0:T(1024)S(1)} %convert_element_type.185) | copy-start | bytes 13828
  504.2 98.4 %reduce-scatter.11.cloned.1.call-start = ((), (), s32[]{:S(2)}) async-start(), calls=%async_computation.20 | async-start | bytes 5898240 | tf_op jit(solution)/shard_map/reduce_scatter | solution.py:28
  517.8 34.4 %copy-start.5 = (f32[2,256,1152]{2,1,0:T(8,128)S(1)}, f32[2,256,1152]{2,1,0:T(8,128)}, u32[]{:S(2)}) copy-start(f32[2,256,1152]{2,1,0:T(8,128)} %copy-done.4) | copy-start | bytes 7077892
  517.8 129.9 %all-gather.23.cloned.1.call-start = ((), (), s32[]{:S(2)}) async-start(), calls=%async_computation.23 | async-start | bytes 5898240 | tf_op jit(solution)/shard_map/all_gather | solution.py:24
  610.1 157.6 %reduce-scatter.21.cloned.1.call-start = ((), (), s32[]{:S(2)}) async-start(), calls=%async_computation.27 | async-start | bytes 2985984 | tf_op jit(solution)/shard_map/reduce_scatter | solution.py:82
  622.2 182.6 %reduce-scatter.23.cloned.1.call-start = ((), (), s32[]{:S(2)}) async-start(), calls=%async_computation.28 | async-start | bytes 2985984 | tf_op jit(solution)/shard_map/reduce_scatter | solution.py:82
  636.4 217.0 %reduce-scatter.15.cloned.1.call-start = ((), (), s32[]{:S(2)}) async-start(), calls=%async_computation.24 | async-start | bytes 5898240 | tf_op jit(solution)/shard_map/reduce_scatter | solution.py:28
  759.2 47.6 %all-to-all-start.2 = ((bf16[2,256,1152]{2,0,1:T(2,128)(2,1)}), bf16[2,256,1152]{2,0,1:T(2,128)(2,1)S(1)}, u32[]{:S(2)}, u32[]{:S(2)}) async-start(bf16[2,256,1152]{2,0,1:T(2,128)(2,1)} %copy.78), calls=%async_computation.4 | async-start | bytes 2359296 | tf_op jit(solution)/shard_map/all_to_all | solution.py:38
  763.9 169.0 %reduce-scatter.19.cloned.1.call-start = ((), (), s32[]{:S(2)}) async-start(), calls=%async_computation.26 | async-start | bytes 995328 | tf_op jit(solution)/shard_map/reduce_scatter | solution.py:82
  814.4 180.2 %reduce-scatter.17.cloned.1.call-start = ((), (), s32[]{:S(2)}) async-start(), calls=%async_computation.25 | async-start | bytes 2985984 | tf_op jit(solution)/shard_map/reduce_scatter | solution.py:82
  826.4 27.0 %copy-start.3 = (f32[4,2,64,1152]{3,2,0,1:T(8,128)S(1)}, f32[4,2,64,1152]{3,2,0,1:T(8,128)}, u32[]{:S(2)}) copy-start(f32[4,2,64,1152]{3,2,0,1:T(8,128)} %copy-done.2) | copy-start | bytes 7077892
  826.4 27.0 %copy-start.25 = (f32[2,1152]{1,0:T(2,128)S(1)}, f32[2,1152]{1,0:T(2,128)}, u32[]{:S(2)}) copy-start(f32[2,1152]{1,0:T(2,128)} %copy-done.24) | copy-start | bytes 27652
  826.4 27.0 %copy-start.35 = (f32[2,256]{1,0:T(2,128)S(1)}, f32[2,256]{1,0:T(2,128)}, u32[]{:S(2)}) copy-start(f32[2,256]{1,0:T(2,128)} %copy-done.34) | copy-start | bytes 6148
  863.7 9.3 all-to-all-start.5
  873.0 183.8 %all-to-all-start.4 = ((bf16[2,256,1152]{2,0,1:T(2,128)(2,1)}), bf16[2,256,1152]{2,0,1:T(2,128)(2,1)S(1)}, u32[]{:S(2)}, u32[]{:S(2)}) async-start(bf16[2,256,1152]{2,0,1:T(2,128)(2,1)} %copy.83), calls=%async_computation.8 | async-start | bytes 2359296 | tf_op jit(solution)/shard_map/all_to_all | solution.py:38
  880.3 170.2 %copy-start.33 = (bf16[16,144]{1,0:T(8,128)(2,1)S(1)}, bf16[16,144]{1,0:T(8,128)(2,1)}, u32[]{:S(2)}) copy-start(bf16[16,144]{1,0:T(8,128)(2,1)} %copy-done.32) | copy-start | bytes 13828
  880.3 171.4 %copy-start.23 = (f32[16,576]{1,0:T(8,128)S(1)}, f32[16,576]{1,0:T(8,128)}, u32[]{:S(2)}) copy-start(f32[16,576]{1,0:T(8,128)} %copy-done.22) | copy-start | bytes 110596
  880.3 171.4 %copy-start.59 = (s32[16]{0:T(128)S(1)}, s32[16]{0:T(128)}, u32[]{:S(2)}) copy-start(s32[16]{0:T(128)} %param.22) | copy-start | bytes 196
  1029.2 25.0 %copy-start.60 = (s32[16]{0:T(128)S(1)}, s32[16]{0:T(128)}, u32[]{:S(2)}) copy-start(s32[16]{0:T(128)} %param.21) | copy-start | bytes 196
  (49 other events, 177.1 us)
Sparse Core Ops, SparseCore 0:
  32.8 77.0 all-gather.12
  112.0 36.7 all-gather.10
  221.5 47.8 reduce-scatter.8
  271.5 71.1 all-gather.16
  344.8 36.0 all-gather.14
  383.1 55.0 all-gather.18
  440.3 36.0 all-gather.20
  504.3 47.8 reduce-scatter.12
  554.7 47.8 reduce-scatter.10
  610.2 37.4 all-gather.22
  651.8 70.7 reduce-scatter.20
  726.2 78.5 reduce-scatter.22
  807.5 45.7 reduce-scatter.14
  857.2 64.0 reduce-scatter.18
  924.8 69.6 reduce-scatter.16
